TPU v7x, 256 devices: a whole 4x4x8 slice. The times are simulated.
256 devices in a mesh: gx: 16 (over z, x_hi), gy: 8 (over y, x_lo), gz: 2 (over core).
Axes of the slice: x: 4 (x_hi: 2, x_lo: 2; x = x_hi * 2 + x_lo), y: 4, z: 8, core: 2. Of those that a mesh axis runs over, the one named last changes fastest.
Arguments:
- state: float32 [16, 32, 32, 8, 128], P(None, 'gx', 'gy', 'gz'), may hold values from -3 to 3.98, as said below
- bin_count: int32 [32, 32, 8], P('gx', 'gy', 'gz'), may hold values from 0 to 128
- departing: float32 [16, 16, 8, 2, 6, 4, 128], P(None, 'gx', 'gy', 'gz'), may hold values from -3 to 3.98, as said below
- depart_count: int32 [16, 8, 2, 6, 4], P('gx', 'gy', 'gz'), may hold values from 0 to 128, as said below
- depart_block: int32 [16, 8, 2, 6, 4], P('gx', 'gy', 'gz'), may hold values from 0 to 31, as said below
- cut_cell: int32 [16, 8, 2, 512], P('gx', 'gy', 'gz'), may hold values from 0 to 2047
- quad_count: int32 [16, 8, 2, 512], P('gx', 'gy', 'gz'), may hold values from 0 to 8
- wall_id: int32 [16, 8, 2, 512], P('gx', 'gy', 'gz'), may hold values from 0 to 3
- cut_level: float32 [16, 8, 2, 512], P('gx', 'gy', 'gz'), may hold values from -1.5 to 1.5
- wall_normal: float32 [4, 3], replicated, may hold values from -2 to 2
- wall_friction: float32 [4], replicated, may hold values from 0.2 to 1
Outputs:
- moved: float32 [16, 32, 32, 8, 128], P(None, 'gx', 'gy', 'gz')
- arrived: float32 [16, 16, 8, 2, 6, 4, 128], P(None, 'gx', 'gy', 'gz')
Inputs may be any that keep to these rules, and one draw needn't show every extreme that they name: `state`: rows 0 to 2 lie in [0.02, 3.98], row 15 in [0.85, 1.1]. `departing`: rows 0 to 2 lie in [0.02, 3.98], row 15 in [0.85, 1.1]. `depart_count`: zero for bins whose direction leaves the domain across a y or z face. `depart_block`: flat index (x * 4 + y) * 4 + z of a block of the receiving brick on the face the bin enters: x = 0 for +x, x = 1 for -x, likewise y for +y and -y and z for +z and -z. `cut_cell`: flat owned cell index (x * 4 * 4 + y) * 4 * 4 + z of the brick; cells may repeat.
All inputs are finite; a program needn't handle non-finite values.
Results may differ from a plain program's by a relative error of at most 0.0003.
Values sent between devices are 32-bit elements; how exact they have to be, the bound alone decides.
No kernel may reach another device: no remote copies, remote signals or barrier semaphores. Data moves between devices by JAX's collectives and lax.ppermute only.
A program may use at most 128 MiB of HBM per device.

v0:
```python
import jax
import jax.numpy as jnp
import numpy as np
from jax import lax
from jax.experimental import pallas as pl
from jax.experimental.pallas import tpu as pltpu
from jax.sharding import PartitionSpec as P

time_step = 0.1
stiffness = 4.0
gravity = 2.0
flip_ratio = 0.95
mass_floor = 0.25
center = 1.5
quad_points = [
    [0.5, 0.5, 0.5],
    [0.2, 0.7, 0.35],
    [0.8, 0.3, 0.65],
    [0.35, 0.15, 0.85],
    [0.65, 0.85, 0.15],
    [0.1, 0.45, 0.55],
    [0.9, 0.55, 0.45],
    [0.45, 0.9, 0.75],
]
f32 = jnp.float32
bf16 = jnp.bfloat16

ZR = 24
LN = 256
CARRIED = (0, 1, 2, 3, 4, 5, 15)
PARTS = 9
BINROWS = 40
XROWS = 96 + 48 + 48 + BINROWS
YROWS = 96 + 48 + BINROWS
ZROWS = 256 + BINROWS


def lane_iota(shape):
    return lax.broadcasted_iota(jnp.int32, shape, len(shape) - 1)


def sub_iota(shape):
    return lax.broadcasted_iota(jnp.int32, shape, len(shape) - 2)


def spline(coord, nodes):
    distance = jnp.abs(coord - nodes)
    inner = 0.75 - distance * distance
    reach = jnp.maximum(1.5 - distance, 0.0)
    return jnp.where(distance < 0.5, inner, 0.5 * reach * reach)


def parts(value):
    high = value.astype(bf16)
    low = (value - high.astype(f32)).astype(bf16)
    return high, low


def plane_of(wx, wy):
    return jnp.concatenate([wy[y : y + 1] * wx for y in range(8)], axis=0)


def roll_lanes(value, shift):
    return pltpu.roll(value, shift % 128, 1)


def contact_terms(cell_ref, quad_ref, wall_ref, level_ref, normal_ref, friction_ref):
    cells = cell_ref[...]
    counts = quad_ref[...]
    walls = wall_ref[...]
    level = level_ref[...]
    normal = []
    for axis in range(3):
        part = jnp.zeros_like(level)
        for wall in range(4):
            part = jnp.where(walls == wall, normal_ref[wall, axis], part)
        normal.append(part)
    friction = jnp.zeros_like(level)
    for wall in range(4):
        friction = jnp.where(walls == wall, friction_ref[wall], friction)
    inverse = 1.0 / jnp.maximum(counts, 1).astype(f32)
    weights = [None] * 8
    for q, point in enumerate(quad_points):
        level_set = level + (normal[0] * point[0] + normal[1] * point[1] + normal[2] * point[2])
        cover = jnp.clip(0.5 - level_set, 0.0, 1.0)
        share = jnp.where(counts > q, cover * inverse, 0.0)
        for corner in range(8):
            factor = 1.0
            for axis in range(3):
                bit = (corner >> (2 - axis)) & 1
                factor *= point[axis] if bit else 1.0 - point[axis]
            term = share * factor
            weights[corner] = term if weights[corner] is None else weights[corner] + term
    return cells, weights, normal + [friction]


def contact_windows(cell_ref, quad_ref, wall_ref, level_ref, normal_ref, friction_ref):
    cells, weights, factors = contact_terms(
        cell_ref, quad_ref, wall_ref, level_ref, normal_ref, friction_ref
    )
    place_third = cells % 16 + 2 + 4 * lax.axis_index("gz")
    column = (cells // 16) % 16 * 8 + cells // 256
    rows = sub_iota((ZR, 128))
    bit_rows = sub_iota((128, 128))
    lefts_high = []
    lefts_low = []
    rights = []
    for tile in range(4):
        third = place_third[tile : tile + 1]
        first_row = rows == third
        second_row = rows == third + 1
        pieces_high = []
        pieces_low = []
        for pair in range(4):
            lower = weights[2 * pair][tile : tile + 1]
            upper = weights[2 * pair + 1][tile : tile + 1]
            for channel in range(4):
                factor = factors[channel][tile : tile + 1]
                value = jnp.where(
                    first_row, lower * factor, jnp.where(second_row, upper * factor, 0.0)
                )
                high, low = parts(value)
                pieces_high.append(high.astype(f32))
                pieces_low.append(low.astype(f32))
        lefts_high.append(jnp.concatenate(pieces_high, axis=0).astype(bf16))
        lefts_low.append(jnp.concatenate(pieces_low, axis=0).astype(bf16))
        rights.append(
            jnp.where(bit_rows == column[tile : tile + 1], 1.0, 0.0).astype(bf16)
        )
    left = jnp.concatenate(lefts_high + lefts_low, axis=1)
    right = jnp.concatenate(rights + rights, axis=1)
    touched = lax.dot_general(
        left, right, (((1,), (1,)), ((), ())), preferred_element_type=f32
    )
    lanes = lane_iota((4 * ZR, 128))
    first = lanes % 8
    result = [[None, None], [None, None]]
    for pair in range(4):
        dx, dy = pair >> 1, pair & 1
        block = touched[pair * 4 * ZR : (pair + 1) * 4 * ZR]
        near = jnp.where(first <= 5 - dx, block, 0.0)
        far = jnp.where(first >= 6 - dx, block, 0.0)
        for window, (value, shift) in enumerate(
            ((near, 50 + 8 * dy + dx), (far, 46 + 8 * dy + dx))
        ):
            turned = roll_lanes(value, shift)
            for half, piece in enumerate(
                (jnp.where(lanes >= shift, turned, 0.0), jnp.where(lanes < shift, turned, 0.0))
            ):
                known = result[window][half]
                result[window][half] = piece if known is None else known + piece
    return result


def deposit_kernel(*refs):
    inputs, outputs = refs[:11], refs[11:15]
    even = lax.axis_index("gx") % 2 == 0
    copies, (data, total, semaphores) = refs[15:26], refs[26:29]
    window_ref, one_ref, two_ref, bins_ref = refs[29:33]
    sent = []

    def send(place, *where):
        source = refs[29 + place].at[where] if where else refs[29 + place]
        target = outputs[place].at[where] if where else outputs[place]
        sent.append(pltpu.make_async_copy(source, target, semaphores.at[11 + len(sent)]))
        sent[-1].start()

    started = []
    for place in (5, 6, 7, 8, 9, 10, 0, 2, 1, 3, 4):
        started.append(
            pltpu.make_async_copy(inputs[place], copies[place], semaphores.at[place])
        )
        started[-1].start()
    state_ref, bin_count_ref, depart_ref, depart_count_ref, depart_block_ref = copies[:5]
    for window in (0, 3):
        total[window] = jnp.zeros((6, 32, LN), f32)
    for window in (1, 2):
        for third in (0, 5):
            total[window, third] = jnp.zeros((32, LN), f32)
    for copy in started[:6]:
        copy.wait()
    contact = contact_windows(*copies[5:])
    for window in range(2):
        for half in range(2):
            for c in range(4):
                window_ref[window, 4 + c, :, 128 * half : 128 * half + 128] = contact[window][
                    half
                ][ZR * c : ZR * c + ZR]
        send(0, window, slice(4, 8))
    for copy in started[6:]:
        copy.wait()

    core = lax.axis_index("gz")
    plus = bins_of(depart_ref, depart_count_ref, depart_block_ref, 0)
    minus = bins_of(depart_ref, depart_count_ref, depart_block_ref, 1)
    for part in range(PARTS):
        at = 192 + 4 * part
        put_pair(one_ref, two_ref, slice(at, at + 4), even, plus[part], minus[part])
    south = bins_of(depart_ref, depart_count_ref, depart_block_ref, 2)
    north = bins_of(depart_ref, depart_count_ref, depart_block_ref, 3)
    up = bins_of(depart_ref, depart_count_ref, depart_block_ref, 4)
    down = bins_of(depart_ref, depart_count_ref, depart_block_ref, 5)
    for part in range(PARTS):
        bins_ref[4 * part : 4 * part + 4, :] = south[part]
        bins_ref[40 + 4 * part : 44 + 4 * part, :] = north[part]
        bins_ref[80 + 4 * part : 84 + 4 * part, :] = jnp.where(core == 0, up[part], down[part])
    send(1, slice(192, XROWS))
    send(2, slice(192, XROWS))
    send(3)

    size = 8
    groups = [(state_ref, 8 * g, 8 * g) for g in range(4)]
    groups += [(depart_ref, 8 * g, 32 + 8 * g) for g in range(3)]
    for ref, begin, place in groups:
        channel = [ref[c, begin : begin + size, :] for c in range(16)]
        pressure = time_step * 4.0 * stiffness * jnp.maximum(1.0 - channel[15], 0.0)
        spread = [channel[6 + e] + (pressure if e % 4 == 0 else 0.0) for e in range(9)]
        offset = [channel[axis] - center for axis in range(3)]
        for axis in range(3):
            data[axis, place : place + size, :] = channel[axis]
            data[3 + axis, place : place + size, :] = (
                channel[3 + axis]
                - spread[3 * axis] * offset[0]
                - spread[3 * axis + 1] * offset[1]
                - spread[3 * axis + 2] * offset[2]
            )
        for entry in range(9):
            data[6 + entry, place : place + size, :] = spread[entry]

    nodes = sub_iota((8, 128)).astype(f32) - 2.0
    slots = lane_iota((8, 128))
    lanes = lane_iota((32, 128))
    local = lane_iota((8, 128)) % 64
    node_first = (local % 8).astype(f32) - 2.0 - center
    node_second = (local // 8).astype(f32) - 2.0 - center
    node_third = nodes - center

    def one_bin(index, begin, count):
        def row(channel):
            return data[channel, pl.ds(index, 1), :]

        wx = spline(row(0), nodes)
        wy = spline(row(1), nodes)
        wz = jnp.where(slots < count, spline(row(2), nodes), 0.0)
        lifted = jnp.concatenate([wz] + [row(3 + c) * wz for c in range(12)], axis=0)
        lift_high, lift_low = parts(lifted)
        plane_high, plane_low = parts(plane_of(wx, wy))
        left = jnp.concatenate([lift_high, lift_low], axis=1)
        right = jnp.concatenate([plane_high, plane_low], axis=0)
        right = jnp.concatenate([right, right], axis=1)
        moments = lax.dot_general(
            left, right, (((1,), (1,)), ((), ())), preferred_element_type=f32
        )
        sums = [moments[0:8]]
        for axis in range(3):
            at = 32 + 24 * axis
            sums.append(
                moments[8 + 8 * axis : 16 + 8 * axis]
                + moments[at : at + 8] * node_first
                + moments[at + 8 : at + 16] * node_second
                + moments[at + 16 : at + 24] * node_third
            )
        both = jnp.concatenate(sums, axis=0)
        turned = pltpu.roll(both + roll_lanes(both, 64), begin % 128, 1)
        inside = (lanes >= begin) & (lanes < begin + 64)
        beyond = (lanes >= begin - 128) & (lanes < begin - 64)
        return jnp.where(inside, turned, 0.0), jnp.where(beyond, turned, 0.0)

    def residents(step, carry):
        first = step // 4
        third = step % 4
        low, high = None, None
        for second in range(4):
            one, two = one_bin(
                first * 16 + second * 4 + third,
                32 * (second + 1),
                bin_count_ref[first, second, third],
            )
            low = one if low is None else low + one
            high = two if high is None else high + two
        total[first + 1, third + 1, :, 0:128] = low
        total[first + 1, third + 1, :, 128:256] = high
        return carry

    lax.fori_loop(0, 8, residents, 0, unroll=4)

    def leavers(member, carry):
        for direction in range(5):
            block = depart_block_ref[0, 0, 0, member, direction]
            count = depart_count_ref[0, 0, 0, member, direction]
            index = 32 + direction * 4 + member
            window = block // 16 + 1
            begin = 32 * (block // 4 % 4 + 1)
            third = block % 4 + 1
            if direction < 2:
                window = 3 if direction == 0 else 0
            elif direction < 4:
                begin = 160 if direction == 2 else 0
            else:
                block = depart_block_ref[0, 0, 0, member, 4 + core]
                count = depart_count_ref[0, 0, 0, member, 4 + core]
                index = 48 + 4 * core + member
                window = block // 16 + 1
                begin = 32 * (block // 4 % 4 + 1)
                third = 5 - 5 * core
            one, two = one_bin(index, begin, count)
            total[window, third, :, 0:128] += one
            total[window, third, :, 128:256] += two
        return carry

    lax.fori_loop(0, 4, leavers, 0, unroll=4)

    lower_rows = sub_iota((8, 128)) < 4
    lower_lanes = lane_iota((8, 128)) % 8 < 4
    lower_tall = lane_iota((ZR, 128)) % 8 < 4
    leaving = {}
    for half in range(2):
        columns = slice(128 * half, 128 * half + 128)
        for c in range(4):
            folded = []
            for window in range(4):
                piece = [
                    total[window, third + 1 - core, 8 * c : 8 * c + 8, columns]
                    for third in range(5)
                ]
                one = pltpu.roll(piece[1], 4, 0)
                three = pltpu.roll(piece[3], 4, 0)
                folded.append(
                    jnp.concatenate(
                        [
                            piece[0] + jnp.where(lower_rows, 0.0, one),
                            piece[2] + jnp.where(lower_rows, one, three),
                            piece[4] + jnp.where(lower_rows, three, 0.0),
                        ],
                        axis=0,
                    )
                )
            window_ref[0, c, :, columns] = folded[1] + jnp.where(
                lower_tall, roll_lanes(folded[0], -4), 0.0
            )
            window_ref[1, c, :, columns] = folded[2] + jnp.where(
                lower_tall, 0.0, roll_lanes(folded[3], 4)
            )
            leaving[c, half] = (
                folded[3] + jnp.where(lower_tall, roll_lanes(folded[2], -4), 0.0),
                folded[0] + jnp.where(lower_tall, 0.0, roll_lanes(folded[1], 4)),
            )
    send(0, 0, slice(0, 4))
    send(0, 1, slice(0, 4))

    tall = lane_iota((ZR, 128))
    narrow = lane_iota((8, 128))
    for pair in range(2):
        sides = []
        for side, (heavy, light) in enumerate(((pack_lower, pack_upper), (pack_upper, pack_lower))):
            own = [
                heavy(leaving[2 * pair, h][side], leaving[2 * pair + 1, h][side], lower_tall)
                for h in range(2)
            ]
            other = [
                light(leaving[2 * pair, h][side], leaving[2 * pair + 1, h][side], lower_tall)
                for h in range(2)
            ]
            rows_even = slice(2 * pair * ZR, (2 * pair + 1) * ZR)
            rows_odd = slice((2 * pair + 1) * ZR, (2 * pair + 2) * ZR)
            touch = [
                light(contact[1 - side][h][rows_even], contact[1 - side][h][rows_odd], lower_tall)
                for h in range(2)
            ]
            own[1] = jnp.where(tall < 96, own[1], roll_lanes(other[1], 64))
            mixed = jnp.where(tall < 32, other[1], other[0])
            spare = jnp.zeros((8, 128), f32)
            for group in range(6):
                value = touch[1][group // 2 * 8 : group // 2 * 8 + 8]
                swapped = pltpu.roll(value, 4, 0)
                if group % 2 == 0:
                    value = jnp.where(lower_rows, value, swapped)
                else:
                    value = jnp.where(lower_rows, swapped, value)
                inside = (narrow >= 16 * group) & (narrow < 16 * group + 8)
                spare = jnp.where(inside, roll_lanes(value, 16 * group - 48), spare)
            mixed = jnp.concatenate(
                [
                    jnp.where(lower_rows & (core == 1), spare, mixed[0:8]),
                    mixed[8:16],
                    jnp.where(lower_rows | (core == 1), mixed[16:24], spare),
                ],
                axis=0,
            )
            sides.append(own + [mixed, jnp.where(tall >= 48, touch[0], touch[1])])
        places = (2 * pair * ZR, (2 * pair + 1) * ZR, 96 + pair * ZR, 144 + pair * ZR)
        for at, plus, minus in zip(places, *sides):
            put_pair(one_ref, two_ref, slice(at, at + ZR), even, plus, minus)
    send(1, slice(0, 192))
    send(2, slice(0, 192))
    for copy in sent:
        copy.wait()


def bins_of(depart_ref, depart_count_ref, depart_block_ref, direction):
    values = [depart_ref[c, 4 * direction : 4 * direction + 4, :] for c in CARRIED]
    row = sub_iota((4, 128))
    for ref in (depart_count_ref, depart_block_ref):
        value = jnp.zeros((4, 128), jnp.int32)
        for member in range(4):
            value = jnp.where(row == member, ref[0, 0, 0, member, direction], value)
        values.append(value.astype(f32))
    return values


def pack_lower(even_c, odd_c, lower):
    return jnp.where(lower, even_c, roll_lanes(odd_c, 4))


def pack_upper(even_c, odd_c, lower):
    return jnp.where(lower, roll_lanes(even_c, -4), odd_c)


def put_pair(one_ref, two_ref, at, even, plus, minus):
    one_ref[at, :] = jnp.where(even, plus, minus)
    two_ref[at, :] = jnp.where(even, minus, plus)


def take_pair(one_ref, two_ref, at, even):
    one, two = one_ref[at, :], two_ref[at, :]
    return jnp.where(even, two, one), jnp.where(even, one, two)


def stage_kernel(window_in, bins_in, state_ref, window_ref, bins_ref, plane_ref, weight_ref):
    window_ref[...] = window_in[...]
    bins_ref[...] = bins_in[...]
    nodes = sub_iota((8, 128)).astype(f32) - 2.0

    def one_bin(index, carry):
        place = [state_ref[axis, pl.ds(index, 1), :] for axis in range(3)]
        high, low, wz, lever = collect_terms(place, nodes)
        plane_ref[index, 0:64, :] = high
        plane_ref[index, 64:128, :] = low
        weight_ref[index, 0:8, :] = wz
        weight_ref[index, 8:16, :] = lever
        return carry

    lax.fori_loop(0, 32, one_bin, 0, unroll=8)


def collect_terms(place, nodes):
    high, low = parts(plane_of(spline(place[0], nodes), spline(place[1], nodes)))
    wz = spline(place[2], nodes)
    return high, low, wz, wz * (nodes - place[2])


def second_kernel(window_in, from_one, from_two, bins_ref, window_ref, one_ref, two_ref):
    even = lax.axis_index("gx") % 2 == 0
    even_second = lax.axis_index("gy") % 2 == 0
    lanes = lane_iota((ZR, 128))
    lower = lanes % 8 < 4
    core = lax.axis_index("gz")
    narrow = lane_iota((8, 128))
    lower_rows = sub_iota((8, 128)) < 4
    got = [[[None, None], [None, None]] for _ in range(8)]
    for pair in range(2):
        places = (2 * pair * ZR, (2 * pair + 1) * ZR, 96 + pair * ZR, 144 + pair * ZR)
        taken = [take_pair(from_one, from_two, slice(at, at + ZR), even) for at in places]
        for side in range(2):
            own = [taken[0][side], taken[1][side]]
            mixed, touch = taken[2][side], taken[3][side]
            spare = jnp.where(core == 0, mixed[16:24], mixed[0:8])
            swapped = pltpu.roll(spare, 4, 0)
            spare = jnp.where(lower_rows == (core == 1), spare, swapped)
            mixed = jnp.concatenate(
                [
                    jnp.where(lower_rows & (core == 1), 0.0, mixed[0:8]),
                    mixed[8:16],
                    jnp.where(lower_rows | (core == 1), mixed[16:24], 0.0),
                ],
                axis=0,
            )
            other = [
                jnp.where(lanes >= 32, mixed, 0.0),
                jnp.where(
                    lanes < 32, mixed, jnp.where(lanes < 64, roll_lanes(own[1], -64), 0.0)
                ),
            ]
            own[1] = jnp.where(lanes < 96, own[1], 0.0)
            rest = [
                jnp.where(
                    lower_rows,
                    roll_lanes(spare, 48 - 32 * tile),
                    roll_lanes(spare, 32 - 32 * tile),
                )
                for tile in range(3)
            ]
            rest = jnp.concatenate(rest, axis=0)
            touched = [
                jnp.where(lanes >= 48, touch, 0.0),
                jnp.where(lanes < 48, touch, jnp.where(lanes < 56, rest, 0.0)),
            ]
            for half in range(2):
                values = (own[half], other[half]) if side == 0 else (other[half], own[half])
                got[2 * pair][side][half] = jnp.where(lower, values[0], roll_lanes(values[1], 4))
                got[2 * pair + 1][side][half] = jnp.where(
                    lower, roll_lanes(values[0], -4), values[1]
                )
                value = touched[half]
                if side == 0:
                    got[4 + 2 * pair][side][half] = jnp.where(lower, value, 0.0)
                    got[5 + 2 * pair][side][half] = jnp.where(lower, roll_lanes(value, -4), 0.0)
                else:
                    got[4 + 2 * pair][side][half] = jnp.where(lower, 0.0, roll_lanes(value, 4))
                    got[5 + 2 * pair][side][half] = jnp.where(lower, 0.0, value)
    new = [[[None, None], [None, None]] for _ in range(8)]
    for c in range(8):
        for window in range(2):
            for half in range(2):
                columns = slice(128 * half, 128 * half + 128)
                value = window_in[window, c, :, columns] + got[c][window][half]
                new[c][window][half] = value
                window_ref[window, c, :, columns] = value
    for c in range(4):
        near, far = new[c]
        plus = jnp.where(lanes < 64, roll_lanes(near[1], -32), roll_lanes(far[1], 32))
        minus = jnp.where(lanes < 64, near[0], roll_lanes(far[0], 64))
        put_pair(one_ref, two_ref, slice(c * ZR, (c + 1) * ZR), even_second, plus, minus)
    for pair in range(2):
        at = slice(96 + pair * ZR, 96 + (pair + 1) * ZR)
        even_c, odd_c = new[4 + 2 * pair], new[5 + 2 * pair]
        sides = []
        for half in (1, 0):
            sides.append(
                jnp.where(
                    lanes < 64,
                    jnp.where(lanes < 32, roll_lanes(even_c[0][half], -32), even_c[1][half]),
                    jnp.where(
                        lanes < 96, roll_lanes(odd_c[0][half], 32), roll_lanes(odd_c[1][half], 64)
                    ),
                )
            )
        put_pair(one_ref, two_ref, at, even_second, sides[0], sides[1])
    put_pair(
        one_ref, two_ref, slice(144, 184), even_second, bins_ref[0:40, :], bins_ref[40:80, :]
    )


def third_kernel(window_in, from_one, from_two, bins_ref, window_ref, message_ref):
    even = lax.axis_index("gy") % 2 == 0
    core = lax.axis_index("gz")
    lanes = lane_iota((ZR, 128))
    for window in range(2):
        for c in range(8):
            if c < 4:
                near, far = take_pair(from_one, from_two, slice(c * ZR, (c + 1) * ZR), even)
                near = jnp.where(
                    (lanes >= 32) & (lanes < 96),
                    roll_lanes(near, 32 if window == 0 else -32),
                    0.0,
                )
                far = jnp.where(lanes < 64, far if window == 0 else roll_lanes(far, 64), 0.0)
            else:
                at = slice(96 + (c - 4) // 2 * ZR, 96 + ((c - 4) // 2 + 1) * ZR)
                shift = (32, 0, -32, -64)[2 * (c % 2) + window]
                inside = (lanes >= 32) & (lanes < 64)
                near, far = take_pair(from_one, from_two, at, even)
                near = jnp.where(inside, roll_lanes(near, shift), 0.0)
                far = jnp.where(inside, roll_lanes(far, shift), 0.0)
            for half, extra in ((0, near), (1, far)):
                columns = slice(128 * half, 128 * half + 128)
                value = window_in[window, c, :, columns] + extra
                window_ref[window, c, :, columns] = value
                at = ((window * 8 + c) * 2 + half) * 8
                message_ref[at : at + 8, :] = jnp.where(core == 0, value[16:24], value[0:8])
    message_ref[256:296, :] = bins_ref[80:120, :]


def advance(sums):
    mass = jnp.maximum(sums[0], mass_floor)
    previous = [sums[1 + axis] / mass for axis in range(3)]
    velocity = [previous[0], previous[1], previous[2] - time_step * gravity]
    normal = sums[4:7]
    scale = 1.0 + (normal[0] * normal[0] + normal[1] * normal[1] + normal[2] * normal[2])
    dot = velocity[0] * normal[0] + velocity[1] * normal[1] + velocity[2] * normal[2]
    inward = jnp.minimum(dot, 0.0) / scale
    velocity = [velocity[axis] - inward * normal[axis] for axis in range(3)]
    dot = velocity[0] * normal[0] + velocity[1] * normal[1] + velocity[2] * normal[2]
    along = dot / scale
    damp = 1.0 - jnp.exp(-sums[7])
    velocity = [
        velocity[axis] - damp * (velocity[axis] - along * normal[axis]) for axis in range(3)
    ]
    return velocity + previous


def collect_kernel(
    window_in,
    from_z,
    x_one,
    x_two,
    y_one,
    y_two,
    plane_ref,
    weight_ref,
    state_ref,
    bin_count_ref,
    moved_ref,
    arrived_ref,
    data,
    fields,
    turned,
    table,
    picked,
    live,
    target,
    moved,
    arrived,
    semaphores,
):
    core = lax.axis_index("gz")
    row = lax.axis_index("gy")
    lanes = lane_iota((8, 128))
    subs = sub_iota((8, 128))
    lower_rows = subs < 4
    lower_lanes = lanes % 8 < 4

    even_first = lax.axis_index("gx") % 2 == 0
    even_second = lax.axis_index("gy") % 2 == 0
    arrivals = []
    for one_ref, two_ref, begin, even in ((x_one, x_two, 192, even_first), (y_one, y_two, 144, even_second)):
        pairs = [
            take_pair(one_ref, two_ref, slice(begin + 4 * part, begin + 4 * part + 4), even)
            for part in range(PARTS)
        ]
        arrivals += [[pair[0] for pair in pairs], [pair[1] for pair in pairs]]
    arrivals.append([from_z[256 + 4 * part : 260 + 4 * part, :] for part in range(PARTS)])
    for g, values in enumerate(arrivals):
        for part in range(7):
            data[part, 4 * g : 4 * g + 4, :] = values[part]
        slot = lane_iota((4, 128)).astype(f32)
        live[32 + 4 * g : 36 + 4 * g, :] = jnp.where(slot < values[7], 1.0, 0.0)
        block = values[8].astype(jnp.int32)
        for member in range(4):
            target[4 * g + member] = block[member, 0]

    below = core == 0
    above = core == 1
    taken = [
        jnp.logical_not(lower_rows) & above,
        (lower_rows & above) | (jnp.logical_not(lower_rows) & below),
        lower_rows & below,
    ]
    for third in range(3):
        rows = slice(8 * third, 8 * third + 8)
        for half in range(2):
            columns = slice(128 * half, 128 * half + 128)
            sums = [[], []]
            for c in range(8):
                values = [window_in[b, c, rows, columns] for b in range(2)]
                for b in range(2):
                    at = ((b * 8 + c) * 2 + half) * 8
                    edge = pltpu.roll(from_z[at : at + 8, :], 4, 0)
                    values[b] = values[b] + jnp.where(taken[third], edge, 0.0)
                sums[0].append(
                    values[0] + jnp.where(lower_lanes, 0.0, roll_lanes(values[1], 4))
                )
                sums[1].append(
                    values[1] + jnp.where(lower_lanes, roll_lanes(values[0], -4), 0.0)
                )
            node_second = row * 16 + (lanes + 128 * half) // 8 - 6
            node_third = core * 12 + subs + 8 * third - 2
            inside = (
                (node_second >= 0) & (node_second < 128) & (node_third >= 0) & (node_third < 32)
            )
            for b in range(2):
                for c, value in enumerate(advance(sums[b])):
                    fields[b, c, rows, columns] = jnp.where(inside, value, 0.0)

    wide = lane_iota((ZR, 128))
    local = wide % 64
    node_first = (local % 8).astype(f32) - 2.0 - center
    node_second = (local // 8).astype(f32) - 2.0 - center
    for b in range(2):
        for c in range(6):
            low = fields[b, c, :, 0:128]
            high = fields[b, c, :, 128:256]
            shown = [
                jnp.where(wide < 64, roll_lanes(low, -32), roll_lanes(low, 32)),
                jnp.where(wide < 64, roll_lanes(low, 64), low),
                jnp.where(
                    wide < 64,
                    jnp.where(wide < 32, roll_lanes(low, 32), roll_lanes(high, 32)),
                    jnp.where(wide < 96, roll_lanes(low, -32), roll_lanes(high, 96)),
                ),
                jnp.where(wide < 64, high, roll_lanes(high, 64)),
            ]
            for second in range(4):
                turned[second, :, c, :] = shown[second]
                if c < 3:
                    turned[second, :, 6 + c, :] = shown[second] * node_first
                    turned[second, :, 9 + c, :] = shown[second] * node_second
        for second in range(4):
            value = turned[second].reshape(ZR * 16, 128)
            high, low = parts(value)
            table[4 * b + second, :, 0:128] = high
            table[4 * b + second, :, 128:256] = low

    nodes = subs.astype(f32) - 2.0

    def one_bin(index, column, third, high, low, wz, lever):
        right = jnp.concatenate([high, low, high, low], axis=0)
        left = table[column, pl.ds(64 * third, 128), :]
        values = jnp.dot(left, right, preferred_element_type=f32)
        first = values[0:8] * wz[0:1]
        second = values[8:16] * wz[0:1]
        moment = values[0:8] * lever[0:1]
        for k in range(1, 8):
            first = first + values[16 * k : 16 * k + 8] * wz[k : k + 1]
            second = second + values[16 * k + 8 : 16 * k + 16] * wz[k : k + 1]
            moment = moment + values[16 * k : 16 * k + 8] * lever[k : k + 1]
        picked[0:8, index, :] = first
        picked[8:16, index, :] = second
        picked[16:24, index, :] = moment

    def residents(step, carry):
        first = step // 4
        second = step % 4
        for third in range(4):
            index = step * 4 + third
            high, low = plane_ref[index, 0:64, :], plane_ref[index, 64:128, :]
            wz, lever = weight_ref[index, 0:8, :], weight_ref[index, 8:16, :]
            one_bin(index, step, third + core, high, low, wz, lever)
            count = bin_count_ref[first, second, third]
            live[pl.ds(index, 1), :] = jnp.where(lane_iota((1, 128)) < count, 1.0, 0.0)
        return carry

    def movers(step, carry):
        for member in range(4):
            index = 4 * step + member
            block = target[index]
            terms = collect_terms([data[axis, pl.ds(index, 1), :] for axis in range(3)], nodes)
            one_bin(32 + index, block // 4, block % 4 + core, *terms)
        return carry

    lax.fori_loop(0, 5, movers, 0, unroll=5)

    def finish(begin, size, old):
        rows = slice(begin, begin + size)
        valid = live[rows, :]
        got = [picked[c, rows, :] for c in range(19)]
        result = []
        for axis in range(3):
            result.append(old[axis] + time_step * got[axis])
        for axis in range(3):
            result.append(
                flip_ratio * (old[3 + axis] + got[axis] - got[3 + axis])
                + (1.0 - flip_ratio) * got[axis]
            )
        affine = []
        for axis in range(3):
            affine.append(4.0 * (got[6 + axis] - (old[0] - center) * got[axis]))
            affine.append(4.0 * (got[9 + axis] - (old[1] - center) * got[axis]))
            affine.append(4.0 * got[16 + axis])
        result += affine
        result.append(old[6] * (1.0 + time_step * (affine[0] + affine[4] + affine[8])))
        return [value * valid for value in result]

    for g in range(3):
        begin, size = 8 * g, 8 if g < 2 else 4
        rows = slice(begin, begin + size)
        for c, value in enumerate(finish(32 + begin, size, [data[p, rows, :] for p in range(7)])):
            if g < 2:
                arrived[c, rows, :] = value
            else:
                arrived[c, 16:20, :] = jnp.where(core == 1, value, 0.0)
                arrived[c, 20:24, :] = jnp.where(core == 0, value, 0.0)
    arrived_copy = pltpu.make_async_copy(arrived, arrived_ref, semaphores.at[0])
    arrived_copy.start()
    moved_copies = []
    for part in range(2):
        lax.fori_loop(4 * part, 4 * part + 4, residents, 0, unroll=4)
        for g in range(2 * part, 2 * part + 2):
            rows = slice(8 * g, 8 * g + 8)
            for c, value in enumerate(finish(8 * g, 8, [state_ref[c, rows, :] for c in CARRIED])):
                moved[c, rows, :] = value
        where = (slice(None), pl.ds(16 * part, 16))
        moved_copies.append(
            pltpu.make_async_copy(moved.at[where], moved_ref.at[where], semaphores.at[1 + part])
        )
        moved_copies[-1].start()
    arrived_copy.wait()
    for copy in moved_copies:
        copy.wait()


def pairs_along(axis, first, closed):
    count = lax.axis_size(axis)
    route = [(i, (i + 1) % count) for i in range(first, count, 2) if closed or i + 1 < count]
    return route + [(j, i) for i, j in route]


vmem = pl.BlockSpec(memory_space=pltpu.VMEM)
smem = pl.BlockSpec(memory_space=pltpu.SMEM)
limits = pltpu.CompilerParams(vmem_limit_bytes=48 * 1024 * 1024)
ample = pltpu.CompilerParams(vmem_limit_bytes=60 * 1024 * 1024)


def shape_of(*dims):
    return jax.ShapeDtypeStruct(dims, f32)


def body(
    state,
    bin_count,
    departing,
    depart_count,
    depart_block,
    cut_cell,
    quad_count,
    wall_id,
    cut_level,
    wall_normal,
    wall_friction,
):
    state_rows = state.reshape(16, 32, 128)
    leaving = departing.reshape(16, 24, 128)
    cut = [value.reshape(4, 128) for value in (cut_cell, quad_count, wall_id, cut_level)]
    depart_count = jnp.swapaxes(depart_count, 3, 4)
    depart_block = jnp.swapaxes(depart_block, 3, 4)
    operands = (
        state_rows,
        bin_count,
        leaving,
        depart_count,
        depart_block,
        *cut,
        wall_normal,
        wall_friction,
    )
    scalars = (1, 3, 4, 9, 10)
    window, one, two, bins = pl.pallas_call(
        deposit_kernel,
        out_shape=[
            shape_of(2, 8, ZR, LN),
            shape_of(XROWS, 128),
            shape_of(XROWS, 128),
            shape_of(3 * BINROWS, 128),
        ],
        in_specs=[pl.BlockSpec(memory_space=pltpu.HBM)] * 11,
        out_specs=[pl.BlockSpec(memory_space=pltpu.HBM)] * 4,
        scratch_shapes=[
            (pltpu.SMEM if place in scalars else pltpu.VMEM)(value.shape, value.dtype)
            for place, value in enumerate(operands)
        ]
        + [
            pltpu.VMEM((16, 56, 128), f32),
            pltpu.VMEM((4, 6, 32, LN), f32),
            pltpu.SemaphoreType.DMA((20,)),
            pltpu.VMEM((2, 8, ZR, LN), f32),
            pltpu.VMEM((XROWS, 128), f32),
            pltpu.VMEM((XROWS, 128), f32),
            pltpu.VMEM((3 * BINROWS, 128), f32),
        ],
        compiler_params=ample,
        name="deposit",
    )(*operands)
    x_one = lax.ppermute(one, "gx", pairs_along("gx", 0, True))
    x_two = lax.ppermute(two, "gx", pairs_along("gx", 1, True))
    window, bins, planes, weights = pl.pallas_call(
        stage_kernel,
        out_shape=[
            shape_of(2, 8, ZR, LN),
            shape_of(3 * BINROWS, 128),
            jax.ShapeDtypeStruct((32, 128, 128), bf16),
            shape_of(32, 16, 128),
        ],
        in_specs=[vmem] * 3,
        out_specs=[vmem] * 4,
        cost_estimate=pl.CostEstimate(flops=10**9, bytes_accessed=2**20, transcendentals=0),
        compiler_params=limits,
        name="stage",
    )(window, bins, state_rows)
    window, one, two = pl.pallas_call(
        second_kernel,
        out_shape=[shape_of(2, 8, ZR, LN), shape_of(YROWS, 128), shape_of(YROWS, 128)],
        in_specs=[vmem] * 4,
        out_specs=[vmem] * 3,
        compiler_params=limits,
        name="take_x",
    )(window, x_one, x_two, bins)
    y_one = lax.ppermute(one, "gy", pairs_along("gy", 0, False))
    y_two = lax.ppermute(two, "gy", pairs_along("gy", 1, False))
    window, message = pl.pallas_call(
        third_kernel,
        out_shape=[shape_of(2, 8, ZR, LN), shape_of(ZROWS, 128)],
        in_specs=[vmem] * 4,
        out_specs=[vmem] * 2,
        compiler_params=limits,
        name="take_y",
    )(window, y_one, y_two, bins)
    from_z = lax.ppermute(message, "gz", [(0, 1), (1, 0)])
    moved, arrived = pl.pallas_call(
        collect_kernel,
        out_shape=[shape_of(16, 32, 128), shape_of(16, 24, 128)],
        in_specs=[vmem] * 9 + [smem],
        out_specs=[pl.BlockSpec(memory_space=pltpu.HBM)] * 2,
        scratch_shapes=[
            pltpu.VMEM((7, 24, 128), f32),
            pltpu.VMEM((2, 6, ZR, LN), f32),
            pltpu.VMEM((4, ZR, 16, 128), f32),
            pltpu.VMEM((8, ZR * 16, 256), bf16),
            pltpu.VMEM((24, 56, 128), f32),
            pltpu.VMEM((56, 128), f32),
            pltpu.SMEM((20,), jnp.int32),
            pltpu.VMEM((16, 32, 128), f32),
            pltpu.VMEM((16, 24, 128), f32),
            pltpu.SemaphoreType.DMA((3,)),
        ],
        compiler_params=limits,
        name="collect",
    )(
        window,
        from_z,
        x_one,
        x_two,
        y_one,
        y_two,
        planes,
        weights,
        state_rows,
        bin_count,
    )
    return moved.reshape(state.shape), arrived.reshape(departing.shape)


def solution(mesh):
    placed = (
        P(None, "gx", "gy", "gz", None),
        P("gx", "gy", "gz"),
        P(None, "gx", "gy", "gz", None, None, None),
        P("gx", "gy", "gz", None, None),
        P("gx", "gy", "gz", None, None),
        P("gx", "gy", "gz", None),
        P("gx", "gy", "gz", None),
        P("gx", "gy", "gz", None),
        P("gx", "gy", "gz", None),
        P(),
        P(),
    )
    return jax.shard_map(
        body,
        mesh=mesh,
        in_specs=placed,
        out_specs=(P(None, "gx", "gy", "gz", None), P(None, "gx", "gy", "gz", None, None, None)),
        check_vma=False,
    )
```

profile of v0, /device:TPU:17, one launch (start us, length us, event | category | flops | bytes accessed | tf_op | source)
XLA Modules:
  0.0 32.5 jit_solution(7009703969539945505)
XLA Ops:
  0.6 0.0 copy-start
  0.6 4.5 %deposit.1 = (f32[2,8,24,256]{3,2,1,0:T(8,128)}, f32[232,128]{1,0:T(8,128)}, f32[232,128]{1,0:T(8,128)}, f32[120,128]{1,0:T(8,128)}) custom-call(f32[16,32,128]{2,1,0:T(8,128)} %bitcast.12, s32[2,4,4]{2,1,0:T(4,128)} %bin_count_ref.1, f32[16,24,128]{2,1,0:T(8,128)} %bitcast.15, s32[1,1,1,4,6]{4,3,2,1,0:T(4,128)} %bitcast.16, s32[1,1,1,4,6]{4,3,2,1,0:T(4,128)} %bitcast.17, ...), custom_call_target="tpu_custom_call" | custom-call | tf_op jit(solution)/shard_map/deposit/pallas_call | solution.py:837
  5.2 2.8 %collective-permute-start = (f32[232,128]{1,0:T(8,128)}, f32[232,128]{1,0:T(8,128)S(1)}, u32[]{:S(2)}, u32[]{:S(2)}) collective-permute-start(f32[232,128]{1,0:T(8,128)} %get-tuple-element.20), channel_id=1, source_target_pairs={{0,16},{32,48},{64,80},{96,112},{128,144},{160,176},{192,208},{224... | collective-permute-start | bytes 356360 | tf_op jit(solution)/shard_map/ppermute | solution.py:863
  8.0 5.5 %collective-permute-start.1 = (f32[232,128]{1,0:T(8,128)}, f32[232,128]{1,0:T(8,128)S(1)}, u32[]{:S(2)}, u32[]{:S(2)}) collective-permute-start(f32[232,128]{1,0:T(8,128)} %get-tuple-element.21), channel_id=1, source_target_pairs={{16,32},{48,64},{80,96},{112,128},{144,160},{176,192},{208,224},{2... | collective-permute-start | bytes 356360 | tf_op jit(solution)/shard_map/ppermute | solution.py:864
  13.5 0.0 copy-done
  13.5 0.0 copy-start.2
  13.6 1.0 %copy-done.2 = f32[2,8,24,256]{3,2,1,0:T(8,128)S(1)} copy-done((f32[2,8,24,256]{3,2,1,0:T(8,128)S(1)}, f32[2,8,24,256]{3,2,1,0:T(8,128)}, u32[]{:S(2)}) %copy-start.2) | copy-done | bytes 393240
  14.5 0.0 copy-start.3
  14.5 0.8 %copy-done.3 = f32[120,128]{1,0:T(8,128)S(1)} copy-done((f32[120,128]{1,0:T(8,128)S(1)}, f32[120,128]{1,0:T(8,128)}, u32[]{:S(2)}) %copy-start.3) | copy-done | bytes 61464
  15.4 0.3 %stage.1 = (f32[2,8,24,256]{3,2,1,0:T(8,128)S(1)}, f32[120,128]{1,0:T(8,128)S(1)}, bf16[32,128,128]{2,1,0:T(8,128)(2,1)S(1)}, f32[32,16,128]{2,1,0:T(8,128)S(1)}) custom-call(f32[2,8,24,256]{3,2,1,0:T(8,128)S(1)} %copy-done.2, f32[120,128]{1,0:T(8,128)S(1)} %copy-done.3, f32[16,32,128]{2,1,0:T(8,128)S(1)} %bitcast.13), custom_call_target="tpu_custom_call" | custom-call | flops 1000000000 | bytes 1048576 | tf_op jit(solution)/shard_map/stage/pallas_call | solution.py:865
  15.7 0.0 collective-permute-done.from_one.x_one
  15.7 0.7 %collective-permute-done.1.from_two.x_two = f32[232,128]{1,0:T(8,128)S(1)} collective-permute-done((f32[232,128]{1,0:T(8,128)}, f32[232,128]{1,0:T(8,128)S(1)}, u32[]{:S(2)}, u32[]{:S(2)}) %collective-permute-start.1) | collective-permute-done | bytes 118816 | tf_op jit(solution)/shard_map/ppermute | solution.py:864
  16.4 0.3 %take_x.1 = (f32[2,8,24,256]{3,2,1,0:T(8,128)S(1)}, f32[184,128]{1,0:T(8,128)S(1)}, f32[184,128]{1,0:T(8,128)S(1)}) custom-call(f32[2,8,24,256]{3,2,1,0:T(8,128)S(1)} %get-tuple-element.19.window_in, f32[232,128]{1,0:T(8,128)S(1)} %collective-permute-done.from_one.x_one, f32[232,128]{1,0:T(8,128)S(1)} %collective-permute-done.1.from_two.x_two, ...), custom_call_target="tpu_custom_call" | custom-call | tf_op jit(solution)/shard_map/take_x/pallas_call | solution.py:879
  16.7 1.3 %collective-permute-start.2 = (f32[184,128]{1,0:T(8,128)S(1)}, f32[184,128]{1,0:T(8,128)S(1)}, u32[]{:S(2)}, u32[]{:S(2)}) collective-permute-start(f32[184,128]{1,0:T(8,128)S(1)} %get-tuple-element.24), channel_id=1, source_target_pairs={{0,2},{4,6},{8,10},{12,14},{2,0},{6,4},{10,8},{14,12},{1,3},{5,7},... | collective-permute-start | bytes 282632 | tf_op jit(solution)/shard_map/ppermute | solution.py:887
  18.0 2.0 %collective-permute-start.3 = (f32[184,128]{1,0:T(8,128)S(1)}, f32[184,128]{1,0:T(8,128)S(1)}, u32[]{:S(2)}, u32[]{:S(2)}) collective-permute-start(f32[184,128]{1,0:T(8,128)S(1)} %get-tuple-element.25), channel_id=1, source_target_pairs={{2,4},{6,8},{10,12},{4,2},{8,6},{12,10},{3,5},{7,9},{11,13},{5,3},... | collective-permute-start | bytes 282632 | tf_op jit(solution)/shard_map/ppermute | solution.py:888
  20.1 0.2 collective-permute-done.2.from_one.y_one
  20.3 4.0 %collective-permute-done.3.from_two.y_two = f32[184,128]{1,0:T(8,128)S(1)} collective-permute-done((f32[184,128]{1,0:T(8,128)S(1)}, f32[184,128]{1,0:T(8,128)S(1)}, u32[]{:S(2)}, u32[]{:S(2)}) %collective-permute-start.3) | collective-permute-done | bytes 94240 | tf_op jit(solution)/shard_map/ppermute | solution.py:888
  24.2 0.2 take_y.1
  24.4 0.0 copy-start.1
  24.4 3.2 %collective-permute-start.4 = (f32[296,128]{1,0:T(8,128)S(1)}, f32[296,128]{1,0:T(8,128)S(1)}, u32[]{:S(2)}, u32[]{:S(2)}) collective-permute-start(f32[296,128]{1,0:T(8,128)S(1)} %get-tuple-element.27), channel_id=1, source_target_pairs={{0,1},{1,0},{2,3},{3,2},{4,5},{5,4},{6,7},{7,6},{8,9},{9,8},{10,11... | collective-permute-start | bytes 454664 | tf_op jit(solution)/shard_map/ppermute | solution.py:897
  27.6 1.0 %collective-permute-done.4.from_z = f32[296,128]{1,0:T(8,128)S(1)} collective-permute-done((f32[296,128]{1,0:T(8,128)S(1)}, f32[296,128]{1,0:T(8,128)S(1)}, u32[]{:S(2)}, u32[]{:S(2)}) %collective-permute-start.4) | collective-permute-done | bytes 151584 | tf_op jit(solution)/shard_map/ppermute | solution.py:897
  28.6 0.0 copy-done.1
  28.6 3.9 %collect.1 = (f32[16,32,128]{2,1,0:T(8,128)}, f32[16,24,128]{2,1,0:T(8,128)}) custom-call(f32[2,8,24,256]{3,2,1,0:T(8,128)S(1)} %get-tuple-element.26.window_in, f32[296,128]{1,0:T(8,128)S(1)} %collective-permute-done.4.from_z, f32[232,128]{1,0:T(8,128)S(1)} %collective-permute-done.from_one.x_one, f32[232,128]{1,0:T(8,128)S(1)} %collective-permute-done.1.from_two.x_two, ...), custom_call_target="tpu_custom_call" | custom-call | tf_op jit(solution)/shard_map/collect/pallas_call | solution.py:898
Async XLA Ops:
  0.6 12.9 %copy-start = (f32[16,2,4,4,128]{4,3,2,1,0:T(4,128)S(1)}, f32[16,2,4,4,128]{4,3,2,1,0:T(4,128)}, u32[]{:S(2)}) copy-start(f32[16,2,4,4,128]{4,3,2,1,0:T(4,128)} %param.11) | copy-start | bytes 786436
  5.2 10.5 %collective-permute-start = (f32[232,128]{1,0:T(8,128)}, f32[232,128]{1,0:T(8,128)S(1)}, u32[]{:S(2)}, u32[]{:S(2)}) collective-permute-start(f32[232,128]{1,0:T(8,128)} %get-tuple-element.20), channel_id=1, source_target_pairs={{0,16},{32,48},{64,80},{96,112},{128,144},{160,176},{192,208},{224... | collective-permute-start | bytes 356360 | tf_op jit(solution)/shard_map/ppermute | solution.py:863
  8.0 8.4 %collective-permute-start.1 = (f32[232,128]{1,0:T(8,128)}, f32[232,128]{1,0:T(8,128)S(1)}, u32[]{:S(2)}, u32[]{:S(2)}) collective-permute-start(f32[232,128]{1,0:T(8,128)} %get-tuple-element.21), channel_id=1, source_target_pairs={{16,32},{48,64},{80,96},{112,128},{144,160},{176,192},{208,224},{2... | collective-permute-start | bytes 356360 | tf_op jit(solution)/shard_map/ppermute | solution.py:864
  13.5 1.0 %copy-start.2 = (f32[2,8,24,256]{3,2,1,0:T(8,128)S(1)}, f32[2,8,24,256]{3,2,1,0:T(8,128)}, u32[]{:S(2)}) copy-start(f32[2,8,24,256]{3,2,1,0:T(8,128)} %get-tuple-element.17.window_in) | copy-start | bytes 1179652
  14.5 0.8 %copy-start.3 = (f32[120,128]{1,0:T(8,128)S(1)}, f32[120,128]{1,0:T(8,128)}, u32[]{:S(2)}) copy-start(f32[120,128]{1,0:T(8,128)} %get-tuple-element.18.bins_in) | copy-start | bytes 184324
  16.7 3.5 %collective-permute-start.2 = (f32[184,128]{1,0:T(8,128)S(1)}, f32[184,128]{1,0:T(8,128)S(1)}, u32[]{:S(2)}, u32[]{:S(2)}) collective-permute-start(f32[184,128]{1,0:T(8,128)S(1)} %get-tuple-element.24), channel_id=1, source_target_pairs={{0,2},{4,6},{8,10},{12,14},{2,0},{6,4},{10,8},{14,12},{1,3},{5,7},... | collective-permute-start | bytes 282632 | tf_op jit(solution)/shard_map/ppermute | solution.py:887
  18.0 6.2 %collective-permute-start.3 = (f32[184,128]{1,0:T(8,128)S(1)}, f32[184,128]{1,0:T(8,128)S(1)}, u32[]{:S(2)}, u32[]{:S(2)}) collective-permute-start(f32[184,128]{1,0:T(8,128)S(1)} %get-tuple-element.25), channel_id=1, source_target_pairs={{2,4},{6,8},{10,12},{4,2},{8,6},{12,10},{3,5},{7,9},{11,13},{5,3},... | collective-permute-start | bytes 282632 | tf_op jit(solution)/shard_map/ppermute | solution.py:888
  24.4 4.2 %copy-start.1 = (s32[2,4,4]{2,1,0:T(4,128)S(1)}, s32[2,4,4]{2,1,0:T(4,128)}, u32[]{:S(2)}) copy-start(s32[2,4,4]{2,1,0:T(4,128)} %bin_count_ref.1) | copy-start | bytes 388
  24.4 4.2 %collective-permute-start.4 = (f32[296,128]{1,0:T(8,128)S(1)}, f32[296,128]{1,0:T(8,128)S(1)}, u32[]{:S(2)}, u32[]{:S(2)}) collective-permute-start(f32[296,128]{1,0:T(8,128)S(1)} %get-tuple-element.27), channel_id=1, source_target_pairs={{0,1},{1,0},{2,3},{3,2},{4,5},{5,4},{6,7},{7,6},{8,9},{9,8},{10,11... | collective-permute-start | bytes 454664 | tf_op jit(solution)/shard_map/ppermute | solution.py:897
where the time goes:
time: 32.7 us; the launch traced here: 32.5 us
  starting transfers between devices  14.9 us (46%)
  Pallas kernels  9.32 us (29%)
  waiting for transfers between devices  5.83 us (18%)
  local copies, waits for them, and re-layouts  1.83 us (6%)
  between operations  0.7 us (2%)
    ppermute x1, starting transfers between devices, body(): x_two = lax.ppermute(two, 'gx', pairs_along('gx', 1, True))  5.52 us
    pallas_call x1, Pallas kernels, body(): pl.pallas_call(deposit_kernel, out_shape=[shape_of(2, 8, ZR, LN), shape_o...  4.54 us
    ppermute x1, waiting for transfers between devices, body(): y_two = lax.ppermute(two, 'gy', pairs_along('gy', 1, False))  3.99 us
    pallas_call x1, Pallas kernels, body(): pl.pallas_call(collect_kernel, out_shape=[shape_of(16, 32, 128), shape_of...  3.93 us
    ppermute x1, starting transfers between devices, body(): from_z = lax.ppermute(message, 'gz', [(0, 1), (1, 0)])  3.17 us
    ppermute x1, starting transfers between devices, body(): x_one = lax.ppermute(one, 'gx', pairs_along('gx', 0, True))  2.84 us
    ppermute x1, starting transfers between devices, body(): y_two = lax.ppermute(two, 'gy', pairs_along('gy', 1, False))  2.04 us
    unnamed x8, local copies, waits for them, and re-layouts  1.83 us
  transfers between devices with their start and end apart: 5, of which 4 were waited for; matrix products, arithmetic and copies ran while one was open for 0% of the time, Pallas kernels for 1%

commit v1 on v0

--- a/solution.py
+++ b/solution.py
@@ -153,17 +153,9 @@
 
 
 def deposit_kernel(*refs):
-    inputs, outputs = refs[:11], refs[11:15]
+    inputs, (window_ref, one_ref, two_ref, bins_ref) = refs[:11], refs[11:15]
     even = lax.axis_index("gx") % 2 == 0
-    copies, (data, total, semaphores) = refs[15:26], refs[26:29]
-    window_ref, one_ref, two_ref, bins_ref = refs[29:33]
-    sent = []
-
-    def send(place, *where):
-        source = refs[29 + place].at[where] if where else refs[29 + place]
-        target = outputs[place].at[where] if where else outputs[place]
-        sent.append(pltpu.make_async_copy(source, target, semaphores.at[11 + len(sent)]))
-        sent[-1].start()
+    copies, (data, total, semaphores) = refs[15:26], refs[26:]
 
     started = []
     for place in (5, 6, 7, 8, 9, 10, 0, 2, 1, 3, 4):
@@ -186,7 +178,6 @@
                 window_ref[window, 4 + c, :, 128 * half : 128 * half + 128] = contact[window][
                     half
                 ][ZR * c : ZR * c + ZR]
-        send(0, window, slice(4, 8))
     for copy in started[6:]:
         copy.wait()
 
@@ -204,9 +195,6 @@
         bins_ref[4 * part : 4 * part + 4, :] = south[part]
         bins_ref[40 + 4 * part : 44 + 4 * part, :] = north[part]
         bins_ref[80 + 4 * part : 84 + 4 * part, :] = jnp.where(core == 0, up[part], down[part])
-    send(1, slice(192, XROWS))
-    send(2, slice(192, XROWS))
-    send(3)
 
     size = 8
     groups = [(state_ref, 8 * g, 8 * g) for g in range(4)]
@@ -345,9 +333,6 @@
                 folded[3] + jnp.where(lower_tall, roll_lanes(folded[2], -4), 0.0),
                 folded[0] + jnp.where(lower_tall, 0.0, roll_lanes(folded[1], 4)),
             )
-    send(0, 0, slice(0, 4))
-    send(0, 1, slice(0, 4))
-
     tall = lane_iota((ZR, 128))
     narrow = lane_iota((8, 128))
     for pair in range(2):
@@ -391,10 +376,6 @@
         places = (2 * pair * ZR, (2 * pair + 1) * ZR, 96 + pair * ZR, 144 + pair * ZR)
         for at, plus, minus in zip(places, *sides):
             put_pair(one_ref, two_ref, slice(at, at + ZR), even, plus, minus)
-    send(1, slice(0, 192))
-    send(2, slice(0, 192))
-    for copy in sent:
-        copy.wait()
 
 
 def bins_of(depart_ref, depart_count_ref, depart_block_ref, direction):
@@ -798,7 +779,6 @@
 vmem = pl.BlockSpec(memory_space=pltpu.VMEM)
 smem = pl.BlockSpec(memory_space=pltpu.SMEM)
 limits = pltpu.CompilerParams(vmem_limit_bytes=48 * 1024 * 1024)
-ample = pltpu.CompilerParams(vmem_limit_bytes=60 * 1024 * 1024)
 
 
 def shape_of(*dims):
@@ -833,6 +813,7 @@
         wall_normal,
         wall_friction,
     )
+    operands = tuple(pltpu.with_memory_space_constraint(value, pltpu.HBM) for value in operands)
     scalars = (1, 3, 4, 9, 10)
     window, one, two, bins = pl.pallas_call(
         deposit_kernel,
@@ -843,7 +824,7 @@
             shape_of(3 * BINROWS, 128),
         ],
         in_specs=[pl.BlockSpec(memory_space=pltpu.HBM)] * 11,
-        out_specs=[pl.BlockSpec(memory_space=pltpu.HBM)] * 4,
+        out_specs=[vmem] * 4,
         scratch_shapes=[
             (pltpu.SMEM if place in scalars else pltpu.VMEM)(value.shape, value.dtype)
             for place, value in enumerate(operands)
@@ -851,13 +832,9 @@
         + [
             pltpu.VMEM((16, 56, 128), f32),
             pltpu.VMEM((4, 6, 32, LN), f32),
-            pltpu.SemaphoreType.DMA((20,)),
-            pltpu.VMEM((2, 8, ZR, LN), f32),
-            pltpu.VMEM((XROWS, 128), f32),
-            pltpu.VMEM((XROWS, 128), f32),
-            pltpu.VMEM((3 * BINROWS, 128), f32),
+            pltpu.SemaphoreType.DMA((11,)),
         ],
-        compiler_params=ample,
+        compiler_params=limits,
         name="deposit",
     )(*operands)
     x_one = lax.ppermute(one, "gx", pairs_along("gx", 0, True))

time: 32.7 us -> 31.7 us (0.969)
  local copies, waits for them, and re-layouts: 1.83 us -> 0.01 us
  waiting for transfers between devices: 5.83 us -> 7.44 us
  Pallas kernels: 9.32 us -> 8.55 us
    unnamed x8 -> x4, local copies, waits for them, and re-layouts: 1.83 us -> 0.01 us
    ppermute x1, waiting for transfers between devices: 0.65 us -> 2.26 us  [body(): x_two = lax.ppermute(two, 'gx', pairs_along('gx', 1, True))]
    pallas_call x1, Pallas kernels: 4.54 us -> 3.77 us  [body(): pl.pallas_call(deposit_kernel, out_shape=[shape_of(2, 8, ZR, LN), shape_o...]
where the time goes in v1:
time: 31.7 us; the launch traced here: 31.6 us
  starting transfers between devices  14.9 us (47%)
  Pallas kernels  8.55 us (27%)
  waiting for transfers between devices  7.44 us (23%)
  between operations  0.7 us (2%)
    ppermute x1, starting transfers between devices, body(): x_two = lax.ppermute(two, 'gx', pairs_along('gx', 1, True))  5.51 us
    ppermute x1, waiting for transfers between devices, body(): y_two = lax.ppermute(two, 'gy', pairs_along('gy', 1, False))  4 us
    pallas_call x1, Pallas kernels, body(): pl.pallas_call(collect_kernel, out_shape=[shape_of(16, 32, 128), shape_of...  3.93 us
    pallas_call x1, Pallas kernels, body(): pl.pallas_call(deposit_kernel, out_shape=[shape_of(2, 8, ZR, LN), shape_o...  3.77 us
    ppermute x1, starting transfers between devices, body(): from_z = lax.ppermute(message, 'gz', [(0, 1), (1, 0)])  3.17 us
    ppermute x1, starting transfers between devices, body(): x_one = lax.ppermute(one, 'gx', pairs_along('gx', 0, True))  2.84 us
    ppermute x1, waiting for transfers between devices, body(): x_two = lax.ppermute(two, 'gx', pairs_along('gx', 1, True))  2.26 us
    ppermute x1, starting transfers between devices, body(): y_two = lax.ppermute(two, 'gy', pairs_along('gy', 1, False))  2.04 us
  transfers between devices with their start and end apart: 5, of which 4 were waited for; matrix products, arithmetic and copies ran while one was open for 0% of the time, Pallas kernels for 1%

profile of v1, /device:TPU:17, one launch (start us, length us, event | category | flops | bytes accessed | tf_op | source)
XLA Modules:
  0.0 31.6 jit_solution(14375441252713900857)
XLA Ops:
  0.6 0.0 copy-start
  0.6 3.8 %deposit.1 = (f32[2,8,24,256]{3,2,1,0:T(8,128)S(1)}, f32[232,128]{1,0:T(8,128)S(1)}, f32[232,128]{1,0:T(8,128)S(1)}, f32[120,128]{1,0:T(8,128)S(1)}) custom-call(f32[16,32,128]{2,1,0:T(8,128)} %bitcast.12, s32[2,4,4]{2,1,0:T(4,128)} %bin_count_ref.1, f32[16,24,128]{2,1,0:T(8,128)} %bitcast.15, s32[1,1,1,4,6]{4,3,2,1,0:T(4,128)} %bitcast.16, ...), custom_call_target="tpu_custom_call" | custom-call | tf_op jit(solution)/shard_map/deposit/pallas_call | solution.py:818
  4.4 2.8 %collective-permute-start = (f32[232,128]{1,0:T(8,128)S(1)}, f32[232,128]{1,0:T(8,128)S(1)}, u32[]{:S(2)}, u32[]{:S(2)}) collective-permute-start(f32[232,128]{1,0:T(8,128)S(1)} %get-tuple-element.20), channel_id=1, source_target_pairs={{0,16},{32,48},{64,80},{96,112},{128,144},{160,176},{192,208},{224... | collective-permute-start | bytes 356360 | tf_op jit(solution)/shard_map/ppermute | solution.py:840
  7.3 5.5 %collective-permute-start.1 = (f32[232,128]{1,0:T(8,128)S(1)}, f32[232,128]{1,0:T(8,128)S(1)}, u32[]{:S(2)}, u32[]{:S(2)}) collective-permute-start(f32[232,128]{1,0:T(8,128)S(1)} %get-tuple-element.21), channel_id=1, source_target_pairs={{16,32},{48,64},{80,96},{112,128},{144,160},{176,192},{208,224},{2... | collective-permute-start | bytes 356360 | tf_op jit(solution)/shard_map/ppermute | solution.py:841
  12.8 0.0 copy-done
  12.8 0.3 %stage.1 = (f32[2,8,24,256]{3,2,1,0:T(8,128)S(1)}, f32[120,128]{1,0:T(8,128)S(1)}, bf16[32,128,128]{2,1,0:T(8,128)(2,1)S(1)}, f32[32,16,128]{2,1,0:T(8,128)S(1)}) custom-call(f32[2,8,24,256]{3,2,1,0:T(8,128)S(1)} %get-tuple-element.17.window_in, f32[120,128]{1,0:T(8,128)S(1)} %get-tuple-element.18.bins_in, f32[16,32,128]{2,1,0:T(8,128)S(1)} %bitcast.13), custom_call_target="tpu_custom_call" | custom-call | flops 1000000000 | bytes 1048576 | tf_op jit(solution)/shard_map/stage/pallas_call | solution.py:842
  13.1 0.0 collective-permute-done.from_one.x_one
  13.1 2.3 %collective-permute-done.1.from_two.x_two = f32[232,128]{1,0:T(8,128)S(1)} collective-permute-done((f32[232,128]{1,0:T(8,128)S(1)}, f32[232,128]{1,0:T(8,128)S(1)}, u32[]{:S(2)}, u32[]{:S(2)}) %collective-permute-start.1) | collective-permute-done | bytes 118816 | tf_op jit(solution)/shard_map/ppermute | solution.py:841
  15.4 0.3 %take_x.1 = (f32[2,8,24,256]{3,2,1,0:T(8,128)S(1)}, f32[184,128]{1,0:T(8,128)S(1)}, f32[184,128]{1,0:T(8,128)S(1)}) custom-call(f32[2,8,24,256]{3,2,1,0:T(8,128)S(1)} %get-tuple-element.19.window_in, f32[232,128]{1,0:T(8,128)S(1)} %collective-permute-done.from_one.x_one, f32[232,128]{1,0:T(8,128)S(1)} %collective-permute-done.1.from_two.x_two, ...), custom_call_target="tpu_custom_call" | custom-call | tf_op jit(solution)/shard_map/take_x/pallas_call | solution.py:856
  15.8 1.3 %collective-permute-start.2 = (f32[184,128]{1,0:T(8,128)S(1)}, f32[184,128]{1,0:T(8,128)S(1)}, u32[]{:S(2)}, u32[]{:S(2)}) collective-permute-start(f32[184,128]{1,0:T(8,128)S(1)} %get-tuple-element.24), channel_id=1, source_target_pairs={{0,2},{4,6},{8,10},{12,14},{2,0},{6,4},{10,8},{14,12},{1,3},{5,7},... | collective-permute-start | bytes 282632 | tf_op jit(solution)/shard_map/ppermute | solution.py:864
  17.1 2.0 %collective-permute-start.3 = (f32[184,128]{1,0:T(8,128)S(1)}, f32[184,128]{1,0:T(8,128)S(1)}, u32[]{:S(2)}, u32[]{:S(2)}) collective-permute-start(f32[184,128]{1,0:T(8,128)S(1)} %get-tuple-element.25), channel_id=1, source_target_pairs={{2,4},{6,8},{10,12},{4,2},{8,6},{12,10},{3,5},{7,9},{11,13},{5,3},... | collective-permute-start | bytes 282632 | tf_op jit(solution)/shard_map/ppermute | solution.py:865
  19.1 0.2 collective-permute-done.2.from_one.y_one
  19.3 4.0 %collective-permute-done.3.from_two.y_two = f32[184,128]{1,0:T(8,128)S(1)} collective-permute-done((f32[184,128]{1,0:T(8,128)S(1)}, f32[184,128]{1,0:T(8,128)S(1)}, u32[]{:S(2)}, u32[]{:S(2)}) %collective-permute-start.3) | collective-permute-done | bytes 94240 | tf_op jit(solution)/shard_map/ppermute | solution.py:865
  23.3 0.2 take_y.1
  23.4 0.0 copy-start.1
  23.5 3.2 %collective-permute-start.4 = (f32[296,128]{1,0:T(8,128)S(1)}, f32[296,128]{1,0:T(8,128)S(1)}, u32[]{:S(2)}, u32[]{:S(2)}) collective-permute-start(f32[296,128]{1,0:T(8,128)S(1)} %get-tuple-element.27), channel_id=1, source_target_pairs={{0,1},{1,0},{2,3},{3,2},{4,5},{5,4},{6,7},{7,6},{8,9},{9,8},{10,11... | collective-permute-start | bytes 454664 | tf_op jit(solution)/shard_map/ppermute | solution.py:874
  26.6 1.0 %collective-permute-done.4.from_z = f32[296,128]{1,0:T(8,128)S(1)} collective-permute-done((f32[296,128]{1,0:T(8,128)S(1)}, f32[296,128]{1,0:T(8,128)S(1)}, u32[]{:S(2)}, u32[]{:S(2)}) %collective-permute-start.4) | collective-permute-done | bytes 151584 | tf_op jit(solution)/shard_map/ppermute | solution.py:874
  27.6 0.0 copy-done.1
  27.6 3.9 %collect.1 = (f32[16,32,128]{2,1,0:T(8,128)}, f32[16,24,128]{2,1,0:T(8,128)}) custom-call(f32[2,8,24,256]{3,2,1,0:T(8,128)S(1)} %get-tuple-element.26.window_in, f32[296,128]{1,0:T(8,128)S(1)} %collective-permute-done.4.from_z, f32[232,128]{1,0:T(8,128)S(1)} %collective-permute-done.from_one.x_one, f32[232,128]{1,0:T(8,128)S(1)} %collective-permute-done.1.from_two.x_two, ...), custom_call_target="tpu_custom_call" | custom-call | tf_op jit(solution)/shard_map/collect/pallas_call | solution.py:875
Async XLA Ops:
  0.6 12.1 %copy-start = (f32[16,2,4,4,128]{4,3,2,1,0:T(4,128)S(1)}, f32[16,2,4,4,128]{4,3,2,1,0:T(4,128)}, u32[]{:S(2)}) copy-start(f32[16,2,4,4,128]{4,3,2,1,0:T(4,128)} %param.11) | copy-start | bytes 786436
  4.4 8.7 %collective-permute-start = (f32[232,128]{1,0:T(8,128)S(1)}, f32[232,128]{1,0:T(8,128)S(1)}, u32[]{:S(2)}, u32[]{:S(2)}) collective-permute-start(f32[232,128]{1,0:T(8,128)S(1)} %get-tuple-element.20), channel_id=1, source_target_pairs={{0,16},{32,48},{64,80},{96,112},{128,144},{160,176},{192,208},{224... | collective-permute-start | bytes 356360 | tf_op jit(solution)/shard_map/ppermute | solution.py:840
  7.3 8.1 %collective-permute-start.1 = (f32[232,128]{1,0:T(8,128)S(1)}, f32[232,128]{1,0:T(8,128)S(1)}, u32[]{:S(2)}, u32[]{:S(2)}) collective-permute-start(f32[232,128]{1,0:T(8,128)S(1)} %get-tuple-element.21), channel_id=1, source_target_pairs={{16,32},{48,64},{80,96},{112,128},{144,160},{176,192},{208,224},{2... | collective-permute-start | bytes 356360 | tf_op jit(solution)/shard_map/ppermute | solution.py:841
  15.8 3.5 %collective-permute-start.2 = (f32[184,128]{1,0:T(8,128)S(1)}, f32[184,128]{1,0:T(8,128)S(1)}, u32[]{:S(2)}, u32[]{:S(2)}) collective-permute-start(f32[184,128]{1,0:T(8,128)S(1)} %get-tuple-element.24), channel_id=1, source_target_pairs={{0,2},{4,6},{8,10},{12,14},{2,0},{6,4},{10,8},{14,12},{1,3},{5,7},... | collective-permute-start | bytes 282632 | tf_op jit(solution)/shard_map/ppermute | solution.py:864
  17.1 6.2 %collective-permute-start.3 = (f32[184,128]{1,0:T(8,128)S(1)}, f32[184,128]{1,0:T(8,128)S(1)}, u32[]{:S(2)}, u32[]{:S(2)}) collective-permute-start(f32[184,128]{1,0:T(8,128)S(1)} %get-tuple-element.25), channel_id=1, source_target_pairs={{2,4},{6,8},{10,12},{4,2},{8,6},{12,10},{3,5},{7,9},{11,13},{5,3},... | collective-permute-start | bytes 282632 | tf_op jit(solution)/shard_map/ppermute | solution.py:865
  23.4 4.2 %copy-start.1 = (s32[2,4,4]{2,1,0:T(4,128)S(1)}, s32[2,4,4]{2,1,0:T(4,128)}, u32[]{:S(2)}) copy-start(s32[2,4,4]{2,1,0:T(4,128)} %bin_count_ref.1) | copy-start | bytes 388
  23.5 4.2 %collective-permute-start.4 = (f32[296,128]{1,0:T(8,128)S(1)}, f32[296,128]{1,0:T(8,128)S(1)}, u32[]{:S(2)}, u32[]{:S(2)}) collective-permute-start(f32[296,128]{1,0:T(8,128)S(1)} %get-tuple-element.27), channel_id=1, source_target_pairs={{0,1},{1,0},{2,3},{3,2},{4,5},{5,4},{6,7},{7,6},{8,9},{9,8},{10,11... | collective-permute-start | bytes 454664 | tf_op jit(solution)/shard_map/ppermute | solution.py:874

commit v2 on v1

--- a/solution.py
+++ b/solution.py
@@ -432,7 +432,7 @@
 
 def second_kernel(window_in, from_one, from_two, bins_ref, window_ref, one_ref, two_ref):
     even = lax.axis_index("gx") % 2 == 0
-    even_second = lax.axis_index("gy") % 2 == 0
+    even_second = lax.axis_index("gy") % 2 == 1
     lanes = lane_iota((ZR, 128))
     lower = lanes % 8 < 4
     core = lax.axis_index("gz")
@@ -523,7 +523,7 @@
 
 
 def third_kernel(window_in, from_one, from_two, bins_ref, window_ref, message_ref):
-    even = lax.axis_index("gy") % 2 == 0
+    even = lax.axis_index("gy") % 2 == 1
     core = lax.axis_index("gz")
     lanes = lane_iota((ZR, 128))
     for window in range(2):
@@ -602,7 +602,7 @@
     lower_lanes = lanes % 8 < 4
 
     even_first = lax.axis_index("gx") % 2 == 0
-    even_second = lax.axis_index("gy") % 2 == 0
+    even_second = lax.axis_index("gy") % 2 == 1
     arrivals = []
     for one_ref, two_ref, begin, even in ((x_one, x_two, 192, even_first), (y_one, y_two, 144, even_second)):
         pairs = [
@@ -861,8 +861,8 @@
         compiler_params=limits,
         name="take_x",
     )(window, x_one, x_two, bins)
-    y_one = lax.ppermute(one, "gy", pairs_along("gy", 0, False))
-    y_two = lax.ppermute(two, "gy", pairs_along("gy", 1, False))
+    y_one = lax.ppermute(one, "gy", pairs_along("gy", 1, False))
+    y_two = lax.ppermute(two, "gy", pairs_along("gy", 0, False))
     window, message = pl.pallas_call(
         third_kernel,
         out_shape=[shape_of(2, 8, ZR, LN), shape_of(ZROWS, 128)],

time: 31.7 us -> 32 us (level)
  the two profiles are of different devices: /device:TPU:17 before, /device:TPU:1 now
where the time goes in v2:
time: 32 us; the launch traced here: 31.9 us
  starting transfers between devices  16.5 us (52%)
  Pallas kernels  8.56 us (27%)
  waiting for transfers between devices  6.14 us (19%)
  between operations  0.7 us (2%)
    ppermute x1, starting transfers between devices, body(): x_two = lax.ppermute(two, 'gx', pairs_along('gx', 1, True))  5.52 us
    pallas_call x1, Pallas kernels, body(): pl.pallas_call(collect_kernel, out_shape=[shape_of(16, 32, 128), shape_of...  3.93 us
    ppermute x1, starting transfers between devices, body(): y_two = lax.ppermute(two, 'gy', pairs_along('gy', 0, False))  3.81 us
    pallas_call x1, Pallas kernels, body(): pl.pallas_call(deposit_kernel, out_shape=[shape_of(2, 8, ZR, LN), shape_o...  3.78 us
    ppermute x1, starting transfers between devices, body(): x_one = lax.ppermute(one, 'gx', pairs_along('gx', 0, True))  3.66 us
    ppermute x1, waiting for transfers between devices, body(): y_two = lax.ppermute(two, 'gy', pairs_along('gy', 0, False))  2.85 us
    ppermute x1, starting transfers between devices, body(): from_z = lax.ppermute(message, 'gz', [(0, 1), (1, 0)])  2.8 us
    ppermute x1, waiting for transfers between devices, body(): x_two = lax.ppermute(two, 'gx', pairs_along('gx', 1, True))  2.27 us
  transfers between devices with their start and end apart: 5, of which 3 were waited for; matrix products, arithmetic and copies ran while one was open for 0% of the time, Pallas kernels for 1%

profile of v2, /device:TPU:1, one launch (start us, length us, event | category | flops | bytes accessed | tf_op | source)
XLA Modules:
  0.0 31.9 jit_solution(7884172291745327951)
XLA Ops:
  0.6 0.0 copy-start
  0.6 3.8 %deposit.1 = (f32[2,8,24,256]{3,2,1,0:T(8,128)S(1)}, f32[232,128]{1,0:T(8,128)S(1)}, f32[232,128]{1,0:T(8,128)S(1)}, f32[120,128]{1,0:T(8,128)S(1)}) custom-call(f32[16,32,128]{2,1,0:T(8,128)} %bitcast.12, s32[2,4,4]{2,1,0:T(4,128)} %bin_count_ref.1, f32[16,24,128]{2,1,0:T(8,128)} %bitcast.15, s32[1,1,1,4,6]{4,3,2,1,0:T(4,128)} %bitcast.16, ...), custom_call_target="tpu_custom_call" | custom-call | tf_op jit(solution)/shard_map/deposit/pallas_call | solution.py:818
  4.4 3.7 %collective-permute-start = (f32[232,128]{1,0:T(8,128)S(1)}, f32[232,128]{1,0:T(8,128)S(1)}, u32[]{:S(2)}, u32[]{:S(2)}) collective-permute-start(f32[232,128]{1,0:T(8,128)S(1)} %get-tuple-element.20), channel_id=1, source_target_pairs={{0,16},{32,48},{64,80},{96,112},{128,144},{160,176},{192,208},{224... | collective-permute-start | bytes 356360 | tf_op jit(solution)/shard_map/ppermute | solution.py:840
  8.1 5.5 %collective-permute-start.1 = (f32[232,128]{1,0:T(8,128)S(1)}, f32[232,128]{1,0:T(8,128)S(1)}, u32[]{:S(2)}, u32[]{:S(2)}) collective-permute-start(f32[232,128]{1,0:T(8,128)S(1)} %get-tuple-element.21), channel_id=1, source_target_pairs={{16,32},{48,64},{80,96},{112,128},{144,160},{176,192},{208,224},{2... | collective-permute-start | bytes 356360 | tf_op jit(solution)/shard_map/ppermute | solution.py:841
  13.6 0.0 copy-done
  13.6 0.3 %stage.1 = (f32[2,8,24,256]{3,2,1,0:T(8,128)S(1)}, f32[120,128]{1,0:T(8,128)S(1)}, bf16[32,128,128]{2,1,0:T(8,128)(2,1)S(1)}, f32[32,16,128]{2,1,0:T(8,128)S(1)}) custom-call(f32[2,8,24,256]{3,2,1,0:T(8,128)S(1)} %get-tuple-element.17.window_in, f32[120,128]{1,0:T(8,128)S(1)} %get-tuple-element.18.bins_in, f32[16,32,128]{2,1,0:T(8,128)S(1)} %bitcast.13), custom_call_target="tpu_custom_call" | custom-call | flops 1000000000 | bytes 1048576 | tf_op jit(solution)/shard_map/stage/pallas_call | solution.py:842
  14.0 0.0 collective-permute-done.from_one.x_one
  14.0 2.3 %collective-permute-done.1.from_two.x_two = f32[232,128]{1,0:T(8,128)S(1)} collective-permute-done((f32[232,128]{1,0:T(8,128)S(1)}, f32[232,128]{1,0:T(8,128)S(1)}, u32[]{:S(2)}, u32[]{:S(2)}) %collective-permute-start.1) | collective-permute-done | bytes 118816 | tf_op jit(solution)/shard_map/ppermute | solution.py:841
  16.3 0.3 %take_x.1 = (f32[2,8,24,256]{3,2,1,0:T(8,128)S(1)}, f32[184,128]{1,0:T(8,128)S(1)}, f32[184,128]{1,0:T(8,128)S(1)}) custom-call(f32[2,8,24,256]{3,2,1,0:T(8,128)S(1)} %get-tuple-element.19.window_in, f32[232,128]{1,0:T(8,128)S(1)} %collective-permute-done.from_one.x_one, f32[232,128]{1,0:T(8,128)S(1)} %collective-permute-done.1.from_two.x_two, ...), custom_call_target="tpu_custom_call" | custom-call | tf_op jit(solution)/shard_map/take_x/pallas_call | solution.py:856
  16.6 0.7 %collective-permute-start.2 = (f32[184,128]{1,0:T(8,128)S(1)}, f32[184,128]{1,0:T(8,128)S(1)}, u32[]{:S(2)}, u32[]{:S(2)}) collective-permute-start(f32[184,128]{1,0:T(8,128)S(1)} %get-tuple-element.24), channel_id=1, source_target_pairs={{2,4},{6,8},{10,12},{4,2},{8,6},{12,10},{3,5},{7,9},{11,13},{5,3},... | collective-permute-start | bytes 282632 | tf_op jit(solution)/shard_map/ppermute | solution.py:864
  17.3 3.8 %collective-permute-start.3 = (f32[184,128]{1,0:T(8,128)S(1)}, f32[184,128]{1,0:T(8,128)S(1)}, u32[]{:S(2)}, u32[]{:S(2)}) collective-permute-start(f32[184,128]{1,0:T(8,128)S(1)} %get-tuple-element.25), channel_id=1, source_target_pairs={{0,2},{4,6},{8,10},{12,14},{2,0},{6,4},{10,8},{14,12},{1,3},{5,7},... | collective-permute-start | bytes 282632 | tf_op jit(solution)/shard_map/ppermute | solution.py:865
  21.1 0.0 collective-permute-done.2.from_one.y_one
  21.1 2.9 %collective-permute-done.3.from_two.y_two = f32[184,128]{1,0:T(8,128)S(1)} collective-permute-done((f32[184,128]{1,0:T(8,128)S(1)}, f32[184,128]{1,0:T(8,128)S(1)}, u32[]{:S(2)}, u32[]{:S(2)}) %collective-permute-start.3) | collective-permute-done | bytes 94240 | tf_op jit(solution)/shard_map/ppermute | solution.py:865
  23.9 0.2 take_y.1
  24.1 0.0 copy-start.1
  24.1 2.8 %collective-permute-start.4 = (f32[296,128]{1,0:T(8,128)S(1)}, f32[296,128]{1,0:T(8,128)S(1)}, u32[]{:S(2)}, u32[]{:S(2)}) collective-permute-start(f32[296,128]{1,0:T(8,128)S(1)} %get-tuple-element.27), channel_id=1, source_target_pairs={{0,1},{1,0},{2,3},{3,2},{4,5},{5,4},{6,7},{7,6},{8,9},{9,8},{10,11... | collective-permute-start | bytes 454664 | tf_op jit(solution)/shard_map/ppermute | solution.py:874
  26.9 1.0 %collective-permute-done.4.from_z = f32[296,128]{1,0:T(8,128)S(1)} collective-permute-done((f32[296,128]{1,0:T(8,128)S(1)}, f32[296,128]{1,0:T(8,128)S(1)}, u32[]{:S(2)}, u32[]{:S(2)}) %collective-permute-start.4) | collective-permute-done | bytes 151584 | tf_op jit(solution)/shard_map/ppermute | solution.py:874
  27.9 0.0 copy-done.1
  27.9 3.9 %collect.1 = (f32[16,32,128]{2,1,0:T(8,128)}, f32[16,24,128]{2,1,0:T(8,128)}) custom-call(f32[2,8,24,256]{3,2,1,0:T(8,128)S(1)} %get-tuple-element.26.window_in, f32[296,128]{1,0:T(8,128)S(1)} %collective-permute-done.4.from_z, f32[232,128]{1,0:T(8,128)S(1)} %collective-permute-done.from_one.x_one, f32[232,128]{1,0:T(8,128)S(1)} %collective-permute-done.1.from_two.x_two, ...), custom_call_target="tpu_custom_call" | custom-call | tf_op jit(solution)/shard_map/collect/pallas_call | solution.py:875
Async XLA Ops:
  0.6 13.0 %copy-start = (f32[16,2,4,4,128]{4,3,2,1,0:T(4,128)S(1)}, f32[16,2,4,4,128]{4,3,2,1,0:T(4,128)}, u32[]{:S(2)}) copy-start(f32[16,2,4,4,128]{4,3,2,1,0:T(4,128)} %param.11) | copy-start | bytes 786436
  4.4 9.5 %collective-permute-start = (f32[232,128]{1,0:T(8,128)S(1)}, f32[232,128]{1,0:T(8,128)S(1)}, u32[]{:S(2)}, u32[]{:S(2)}) collective-permute-start(f32[232,128]{1,0:T(8,128)S(1)} %get-tuple-element.20), channel_id=1, source_target_pairs={{0,16},{32,48},{64,80},{96,112},{128,144},{160,176},{192,208},{224... | collective-permute-start | bytes 356360 | tf_op jit(solution)/shard_map/ppermute | solution.py:840
  8.1 8.2 %collective-permute-start.1 = (f32[232,128]{1,0:T(8,128)S(1)}, f32[232,128]{1,0:T(8,128)S(1)}, u32[]{:S(2)}, u32[]{:S(2)}) collective-permute-start(f32[232,128]{1,0:T(8,128)S(1)} %get-tuple-element.21), channel_id=1, source_target_pairs={{16,32},{48,64},{80,96},{112,128},{144,160},{176,192},{208,224},{2... | collective-permute-start | bytes 356360 | tf_op jit(solution)/shard_map/ppermute | solution.py:841
  16.6 4.5 %collective-permute-start.2 = (f32[184,128]{1,0:T(8,128)S(1)}, f32[184,128]{1,0:T(8,128)S(1)}, u32[]{:S(2)}, u32[]{:S(2)}) collective-permute-start(f32[184,128]{1,0:T(8,128)S(1)} %get-tuple-element.24), channel_id=1, source_target_pairs={{2,4},{6,8},{10,12},{4,2},{8,6},{12,10},{3,5},{7,9},{11,13},{5,3},... | collective-permute-start | bytes 282632 | tf_op jit(solution)/shard_map/ppermute | solution.py:864
  17.3 6.7 %collective-permute-start.3 = (f32[184,128]{1,0:T(8,128)S(1)}, f32[184,128]{1,0:T(8,128)S(1)}, u32[]{:S(2)}, u32[]{:S(2)}) collective-permute-start(f32[184,128]{1,0:T(8,128)S(1)} %get-tuple-element.25), channel_id=1, source_target_pairs={{0,2},{4,6},{8,10},{12,14},{2,0},{6,4},{10,8},{14,12},{1,3},{5,7},... | collective-permute-start | bytes 282632 | tf_op jit(solution)/shard_map/ppermute | solution.py:865
  24.1 3.8 %copy-start.1 = (s32[2,4,4]{2,1,0:T(4,128)S(1)}, s32[2,4,4]{2,1,0:T(4,128)}, u32[]{:S(2)}) copy-start(s32[2,4,4]{2,1,0:T(4,128)} %bin_count_ref.1) | copy-start | bytes 388
  24.1 3.8 %collective-permute-start.4 = (f32[296,128]{1,0:T(8,128)S(1)}, f32[296,128]{1,0:T(8,128)S(1)}, u32[]{:S(2)}, u32[]{:S(2)}) collective-permute-start(f32[296,128]{1,0:T(8,128)S(1)} %get-tuple-element.27), channel_id=1, source_target_pairs={{0,1},{1,0},{2,3},{3,2},{4,5},{5,4},{6,7},{7,6},{8,9},{9,8},{10,11... | collective-permute-start | bytes 454664 | tf_op jit(solution)/shard_map/ppermute | solution.py:874
